TPU v7x, 512 devices: a whole 4x8x8 slice. The times are simulated.
512 devices in a mesh: sib: 2 (over core), row: 16 (over z, y_lo), col: 16 (over x, y_hi).
Axes of the slice: x: 4, y: 8 (y_hi: 4, y_lo: 2; y = y_hi * 2 + y_lo), z: 8, core: 2. Of those that a mesh axis runs over, the one named last changes fastest.
Arguments:
- child_front: float32 [2, 8192, 8192], P('sib', 'row', 'col'), may hold values from -6 to 6
- child_panel: float32 [2, 8192, 1024], P('sib', ('row', 'col')), may hold values from -0.42 to 0.42
- block_map: int32 [2, 64], replicated, may hold values from 0 to 95, as said below
- parent_front: float32 [12288, 12288], P(('row', 'sib'), 'col'), may hold values from -6 to 6
- pivot_inverse: float32 [512, 512], replicated, may hold values from -0.03 to 0.1, as said below
Outputs:
- parent_out: float32 [12288, 12288], P(('row', 'sib'), 'col')
Inputs may be any that keep to these rules, and one draw needn't show every extreme that they name: `block_map`: each row is strictly increasing. A child block i that lands in parent block g * 6 + k with 0 <= k < 6 satisfies g * 4 - 2 <= i < (g + 1) * 4; the lower end is met for g = 1 in every draw, and the last parent block is always named. `pivot_inverse`: lower triangular with diagonal entries from 0.05 to 0.1.
All inputs are finite; a program needn't handle non-finite values.
Results may differ from a plain program's by a relative error of at most 0.0001.
Values sent between devices are 32-bit elements; how exact they have to be, the bound alone decides.
A program may use at most 64 MiB of HBM per device.

v0:
```python
import jax
import jax.numpy as jnp
from jax import lax
from jax.sharding import Mesh
from jax.sharding import PartitionSpec as P

BLK = 128
CBD = 4
PBD = 6
HB = 2
PANEL = 512
ROW = ("row_0", "row_1")
ROW_COL = ("row_0", "row_1", "col")
ROW_SIB = ("row_0", "row_1", "sib")


def broadcast_by_axis(value, axes, root):
    value = jnp.where(lax.axis_index(axes) == root, value, jnp.zeros_like(value))
    for axis in axes:
        value = lax.psum(value, axis)
    return value


def shifted(value, axis, steps):
    count = lax.axis_size(axis)
    initial, last = (max(0, -steps), min(count, count - steps))
    return lax.ppermute(value, axis, [(source, source + steps) for source in range(initial, last)])


def split_up(value, dim, devices):
    shape = value.shape
    blocks = value.reshape(*shape[:dim], devices, shape[dim] // devices, *shape[dim + 1 :])
    return jnp.moveaxis(blocks, dim, 0)


def summed_on_arrival(value, axis, dim):
    blocks = split_up(value, dim, lax.axis_size(axis))
    arrived = lax.all_to_all(blocks, axis, split_axis=0, concat_axis=0, tiled=True)
    return arrived.sum(axis=0)


def padded_to(lines, devices):
    spare = -len(lines) % devices
    return jnp.pad(lines, [(0, spare)] + [(0, 0)] * (lines.ndim - 1))


def spread(value, axis, root):
    lines = jnp.where(lax.axis_index(axis) == root, value, jnp.zeros_like(value)).reshape(
        -1, *value.shape[1:][-1:]
    )
    padded = padded_to(lines, lax.axis_size(axis))
    own = lax.psum_scatter(padded, axis, scatter_dimension=0, tiled=True)
    return lax.all_gather(own, axis, axis=0, tiled=True)[: len(lines)].reshape(value.shape)


def from_everyone(value, axis):
    devices = lax.axis_size(axis)
    return lax.all_to_all(
        jnp.broadcast_to(value[None], (devices, *value.shape)), axis, 0, 0, tiled=True
    )


def joined_along(blocks, dim):
    shape = list(blocks.shape[1:])
    shape[dim] *= blocks.shape[0]
    return jnp.moveaxis(blocks, 0, dim).reshape(shape)


def collect(value, axis, dim):
    blocks = from_everyone(value, axis)
    return joined_along(blocks, dim)


def choose_blocks(block_row, device, child_span, parent_span, edge_span):
    padded = jnp.concatenate([jnp.full((edge_span,), -1, jnp.int32), block_row])
    window = lax.dynamic_slice_in_dim(padded, device * child_span, child_span + edge_span)
    target = device * parent_span + jnp.arange(parent_span, dtype=jnp.int32)
    return (window[None, :] == target[:, None]).astype(jnp.float32)


def times_inverse(rows_part, pivot_inverse):
    return lax.dot_general(
        rows_part,
        pivot_inverse,
        (((1,), (1,)), ((), ())),
        precision=lax.Precision.HIGHEST,
        preferred_element_type=jnp.float32,
    )


def shards(child_front, child_panel, block_map, parent_front, pivot_inverse):
    front_index = lax.axis_index("sib")
    row_index = lax.axis_index(ROW)
    col_index = lax.axis_index("col")
    child_rows = child_front.shape[1]
    parent_rows = parent_front.shape[0]
    parent_cols = parent_front.shape[1]
    edge_width = HB * BLK
    span_blocks = CBD + HB
    rows_local = lax.all_gather(child_panel, "col", axis=1, tiled=True)[0]
    cols_local = broadcast_by_axis(rows_local, ROW, col_index)
    update = child_front[0] - lax.dot_general(
        rows_local,
        cols_local,
        (((1,), (1,)), ((), ())),
        precision=lax.Precision.HIGHEST,
        preferred_element_type=jnp.float32,
    )
    my_map = lax.dynamic_index_in_dim(block_map, front_index, 0, keepdims=False)
    left_cols = shifted(update[:, -edge_width:], "col", 1)
    col_window = jnp.concatenate([left_cols, update], axis=1).reshape(child_rows, span_blocks, BLK)
    col_pick = choose_blocks(my_map, col_index, CBD, PBD, HB)
    spread_cols = jnp.einsum(
        "rwk,qw->rqk", col_window, col_pick, precision=lax.Precision.HIGHEST
    ).reshape(child_rows, PBD * BLK)
    left_rows = shifted(spread_cols[-edge_width:], ROW, 1)
    row_window = jnp.concatenate([left_rows, spread_cols], axis=0).reshape(
        span_blocks, BLK, PBD * BLK
    )
    row_pick = choose_blocks(my_map, row_index, CBD, PBD, HB)
    spread_both = jnp.einsum(
        "wtc,qw->qtc", row_window, row_pick, precision=lax.Precision.HIGHEST
    ).reshape(PBD * BLK, PBD * BLK)
    summed = summed_on_arrival(spread_both, "sib", 0)
    assembled = parent_front + summed
    local_factor = times_inverse(assembled[:, :PANEL], pivot_inverse)
    factor_rows = spread(local_factor, "col", 0)
    owner_rows = broadcast_by_axis(factor_rows, ROW, col_index)
    col_factor = collect(owner_rows, "sib", 0)
    product = lax.dot_general(
        factor_rows,
        col_factor,
        (((1,), (1,)), ((), ())),
        precision=lax.Precision.HIGHEST,
        preferred_element_type=jnp.float32,
    )
    global_rows = (row_index * 2 + front_index) * parent_rows + jnp.arange(
        parent_rows, dtype=jnp.int32
    )
    global_cols = col_index * parent_cols + jnp.arange(parent_cols, dtype=jnp.int32)
    inside = (global_rows[:, None] >= PANEL) & (global_cols[None, :] >= PANEL)
    trailing = jnp.where(inside, assembled - product, assembled)
    factor_wide = jnp.pad(factor_rows, ((0, 0), (0, parent_cols - PANEL)))
    return jnp.where(global_cols[None, :] < PANEL, factor_wide, trailing)


def solution(mesh):
    split = Mesh(
        mesh.devices.reshape(mesh.shape["sib"], 8, 2, mesh.shape["col"]),
        ("sib", "row_0", "row_1", "col"),
    )
    placed = (P("sib", ROW, "col"), P("sib", ROW_COL, None), P(), P(ROW_SIB, "col"), P())
    return jax.shard_map(
        shards, mesh=split, in_specs=placed, out_specs=P(ROW_SIB, "col"), check_vma=False
    )
```

profile of v0, /device:TPU:1, one launch (start us, length us, event | category | flops | bytes accessed | tf_op | source)
XLA Modules:
  0.0 621.0 jit_solution(6062125449259001521)
XLA Ops:
  7.3 72.9 %all-gather.2.cloned.1.call-done = f32[1,512,1024]{2,1,0:T(8,128)} async-done(((f32[1,32,1024]{2,1,0:T(8,128)}), f32[1,512,1024]{2,1,0:T(8,128)}) %all-gather.2.cloned.1.call-update) | async-done | bytes 2097168 | tf_op jit(solution)/shard_map/all_gather | solution.py:100
  80.2 3.2 bitcast_select_fusion
  83.4 82.9 %all-reduce.7.cloned.1.call-done = f32[512,1024]{1,0:T(8,128)} async-done(((f32[512,1024]{1,0:T(8,128)}), f32[512,1024]{1,0:T(8,128)}) %all-reduce.7.cloned.1.call-update) | async-done | bytes 2097168 | tf_op jit(solution)/shard_map/psum | solution.py:20
  166.4 2.7 copy.8
  169.1 81.5 %all-reduce.9.cloned.1.call-done = f32[512,1024]{1,0:T(8,128)} async-done(((f32[512,1024]{1,0:T(8,128)}), f32[512,1024]{1,0:T(8,128)}) %all-reduce.9.cloned.1.call-update) | async-done | bytes 2097168 | tf_op jit(solution)/shard_map/psum | solution.py:20
  250.6 5.4 fusion.8
  256.0 1.0 copy-done.2
  257.0 4.1 collective-permute-start
  261.2 13.7 %collective-permute-done = f32[512,256]{0,1:T(8,128)S(1)} collective-permute-done((f32[512,256]{0,1:T(8,128)S(1)}, f32[512,256]{0,1:T(8,128)S(1)}, u32[]{:S(2)}, u32[]{:S(2)}) %collective-permute-start) | collective-permute-done | bytes 524320 | tf_op jit(solution)/shard_map/ppermute | solution.py:27
  275.0 1.3 pad_maximum_fusion.1
  276.3 1.8 copy.9
  278.2 2.7 convolution_bitcast_fusion
  280.8 1.0 slice.17
  281.9 2.4 copy.10
  284.3 11.1 %collective-permute-start.1 = (f32[256,768]{0,1:T(8,128)}, f32[256,768]{0,1:T(8,128)}, u32[]{:S(2)}, u32[]{:S(2)}) collective-permute-start(f32[256,768]{0,1:T(8,128)} %bitcast.40), channel_id=1, source_target_pairs={{0,16},{16,32},{32,48},{48,64},{64,80},{80,96},{96,112},{112,128},... | collective-permute-start | bytes 2359304 | tf_op jit(solution)/shard_map/ppermute | solution.py:27
  295.4 1.6 copy.11
  297.0 13.2 %collective-permute-done.1 = f32[256,768]{0,1:T(8,128)} collective-permute-done((f32[256,768]{0,1:T(8,128)}, f32[256,768]{0,1:T(8,128)}, u32[]{:S(2)}, u32[]{:S(2)}) %collective-permute-start.1) | collective-permute-done | bytes 786464 | tf_op jit(solution)/shard_map/ppermute | solution.py:27
  310.2 3.2 pad_maximum_fusion
  313.4 2.0 copy.12
  315.4 2.9 fusion
  319.1 7.7 %all_to_all.10 = f32[2,384,768]{2,1,0:T(8,128)S(1)} all-to-all(f32[2,384,768]{2,1,0:T(8,128)S(1)} %bitcast.36), channel_id=1, replica_groups=mesh['sib'=2,'row_0'=8,'row_1'=2,'col'=16] {'sib'}, dimensions={0} | all-to-all | bytes 4718592 | tf_op jit(solution)/shard_map/all_to_all | solution.py:38
  326.8 1.3 reduce_sum.9
  328.0 1.8 add.88
  329.8 2.3 convolution_select_fusion
  332.2 94.5 %reduce-scatter.2.cloned.1.call-done = f32[24,512]{1,0:T(8,128)} async-done(((f32[384,512]{1,0:T(8,128)}), f32[24,512]{1,0:T(8,128)}) %reduce-scatter.2.cloned.1.call-update) | async-done | bytes 49168 | tf_op jit(solution)/shard_map/reduce_scatter | solution.py:52
  426.7 41.6 %all_gather.7 = f32[384,512]{1,0:T(8,128)S(1)} all-gather(f32[24,512]{1,0:T(8,128)} %reduce-scatter.2.cloned.1.call-done), channel_id=1, replica_groups=mesh['sib'=2,'row_0'=8,'row_1'=2,'col'=16] {'col'}, dimensions={0}, use_global_device_ids=true | all-gather | bytes 835584 | tf_op jit(solution)/shard_map/all_gather | solution.py:53
  468.3 0.9 broadcast_select_fusion
  469.3 78.7 %all-reduce.11.cloned.1.call-done = f32[384,512]{1,0:T(8,128)} async-done(((f32[384,512]{1,0:T(8,128)}), f32[384,512]{1,0:T(8,128)}) %all-reduce.11.cloned.1.call-update) | async-done | bytes 786448 | tf_op jit(solution)/shard_map/psum | solution.py:20
  548.1 56.2 %all-reduce.13.cloned.1.call-done = f32[384,512]{1,0:T(8,128)} async-done(((f32[384,512]{1,0:T(8,128)}), f32[384,512]{1,0:T(8,128)}) %all-reduce.13.cloned.1.call-update) | async-done | bytes 786448 | tf_op jit(solution)/shard_map/psum | solution.py:20
  604.3 1.3 broadcast_in_dim.11
  605.6 5.3 all_to_all.11
  610.9 3.2 fusion.4
  (27 shorter events, 1.9 us)
Async XLA Ops:
  6.5 323.3 %copy-start = (f32[512,512]{1,0:T(8,128)S(1)}, f32[512,512]{1,0:T(8,128)}, u32[]{:S(2)}) copy-start(f32[512,512]{1,0:T(8,128)} %param.9) | copy-start | bytes 3145732
  6.5 73.6 %all-gather.2.cloned.1.call-start = ((), (), s32[]{:S(2)}) async-start(), calls=%async_computation.3 | async-start | bytes 2228224 | tf_op jit(solution)/shard_map/all_gather | solution.py:100
  7.3 159.1 %all-reduce.7.cloned.1.call-start = ((), (), s32[]{:S(2)}) async-start(), calls=%async_computation.4 | async-start | bytes 4194304 | tf_op jit(solution)/shard_map/psum | solution.py:20
  83.4 167.2 %all-reduce.9.cloned.1.call-start = ((), (), s32[]{:S(2)}) async-start(), calls=%async_computation.5 | async-start | bytes 4194304 | tf_op jit(solution)/shard_map/psum | solution.py:20
  166.4 84.2 %copy-start.1 = (f32[1,512,1024]{2,1,0:T(8,128)S(1)}, f32[1,512,1024]{2,1,0:T(8,128)}, u32[]{:S(2)}) copy-start(f32[1,512,1024]{2,1,0:T(8,128)} %all-gather.2.cloned.1.call-done) | copy-start | bytes 6291460
  166.4 260.3 %reduce-scatter.2.cloned.1.call-start = ((), (), s32[]{:S(2)}) async-start(), calls=%async_computation.6 | async-start | bytes 835584 | tf_op jit(solution)/shard_map/reduce_scatter | solution.py:52
  169.1 92.0 %copy-start.3 = (s32[2,64]{1,0:T(2,128)S(1)}, s32[2,64]{1,0:T(2,128)}, u32[]{:S(2)}) copy-start(s32[2,64]{1,0:T(2,128)} %param.7) | copy-start | bytes 1540
  256.0 1.0 copy-start.2
  257.0 17.9 %collective-permute-start = (f32[512,256]{0,1:T(8,128)S(1)}, f32[512,256]{0,1:T(8,128)S(1)}, u32[]{:S(2)}, u32[]{:S(2)}) collective-permute-start(f32[512,256]{0,1:T(8,128)S(1)} %slice.16), channel_id=1, source_target_pairs={{0,1},{1,2},{2,3},{3,4},{4,5},{5,6},{6,7},{7,8},{8,9},{9,10},{10,1... | collective-permute-start | bytes 1572872 | tf_op jit(solution)/shard_map/ppermute | solution.py:27
  284.3 25.9 %collective-permute-start.1 = (f32[256,768]{0,1:T(8,128)}, f32[256,768]{0,1:T(8,128)}, u32[]{:S(2)}, u32[]{:S(2)}) collective-permute-start(f32[256,768]{0,1:T(8,128)} %bitcast.40), channel_id=1, source_target_pairs={{0,16},{16,32},{32,48},{48,64},{64,80},{80,96},{96,112},{112,128},... | collective-permute-start | bytes 2359304 | tf_op jit(solution)/shard_map/ppermute | solution.py:27
  332.2 215.8 %all-reduce.11.cloned.1.call-start = ((), (), s32[]{:S(2)}) async-start(), calls=%async_computation.7 | async-start | bytes 1572864 | tf_op jit(solution)/shard_map/psum | solution.py:20
  469.2 135.1 %all-reduce.13.cloned.1.call-start = ((), (), s32[]{:S(2)}) async-start(), calls=%async_computation.8 | async-start | bytes 1572864 | tf_op jit(solution)/shard_map/psum | solution.py:20
Sparse Core Ops, SparseCore 0:
  10.4 69.7 all-gather.1
  83.5 82.8 all-reduce.6
  169.3 81.2 all-reduce.8
  332.3 94.3 reduce-scatter.1
  469.3 78.6 all-reduce.10
  550.7 53.5 all-reduce.12
where the time goes:
time: 621 us
  waiting for transfers between devices  494 us (80%)
  blocking collectives  54.5 us (9%)
  matrix products  16.5 us (3%)
  starting transfers between devices  15.4 us (2%)
  local copies, waits for them, and re-layouts  14.8 us (2%)
  between operations  13.6 us (2%)
  other arithmetic  11.7 us (2%)
    psum x4, waiting for transfers between devices, broadcast_by_axis(): value = lax.psum(value, axis)  299 us
    reduce_scatter x1, waiting for transfers between devices, spread(): own = lax.psum_scatter(padded, axis, scatter_dimension=0, tiled=True)  94.5 us
    all_gather x1, waiting for transfers between devices, shards(): rows_local = lax.all_gather(child_panel, 'col', axis=1, tiled=True)[0]  72.9 us
    all_gather x1, blocking collectives, spread(): lax.all_gather(own, axis, axis=0, tiled=True)[:len(lines)]  41.6 us
    ppermute x2, waiting for transfers between devices, shifted(): lax.ppermute(value, axis, [(source, source + steps) for source in range(i...  26.9 us
    ppermute x2, starting transfers between devices, shifted(): lax.ppermute(value, axis, [(source, source + steps) for source in range(i...  15.2 us
  transfers between devices with their start and end apart: 8, of which 8 were waited for; matrix products, arithmetic and copies ran while one was open for 1% of the time, Pallas kernels for 0%

commit v1 on v0

--- a/solution.py
+++ b/solution.py
@@ -97,7 +97,9 @@
     parent_cols = parent_front.shape[1]
     edge_width = HB * BLK
     span_blocks = CBD + HB
-    rows_local = lax.all_gather(child_panel, "col", axis=1, tiled=True)[0]
+    rows_local = jnp.concatenate(
+        lax.all_to_all(jnp.stack([child_panel] * lax.axis_size("col")), "col", 0, 0), axis=1
+    )[0]
     cols_local = broadcast_by_axis(rows_local, ROW, col_index)
     update = child_front[0] - lax.dot_general(
         rows_local,

time: 621 us -> 613 us (0.987)
  waiting for transfers between devices: 494 us -> 475 us
  starting transfers between devices: 15.4 us -> 25.6 us
    all_gather x1 -> x0, waiting for transfers between devices: 72.9 us -> none  [shards(): rows_local = lax.all_gather(child_panel, 'col', axis=1, tiled=True)[0]]
    all_to_all x0 -> x1, waiting for transfers between devices: none -> 49.6 us  [shards(): lax.all_to_all(jnp.stack([child_panel] * lax.axis_size('col')), 'col', 0, 0)]
    all_to_all x0 -> x1, starting transfers between devices: none -> 10.2 us  [shards(): lax.all_to_all(jnp.stack([child_panel] * lax.axis_size('col')), 'col', 0, 0)]
where the time goes in v1:
time: 613 us
  waiting for transfers between devices  475 us (77%)
  blocking collectives  54.5 us (9%)
  starting transfers between devices  25.6 us (4%)
  local copies, waits for them, and re-layouts  17.3 us (3%)
  matrix products  16.5 us (3%)
  between operations  13.3 us (2%)
  other arithmetic  10 us (2%)
    psum x4, waiting for transfers between devices, broadcast_by_axis(): value = lax.psum(value, axis)  304 us
    reduce_scatter x1, waiting for transfers between devices, spread(): own = lax.psum_scatter(padded, axis, scatter_dimension=0, tiled=True)  94.5 us
    all_to_all x1, waiting for transfers between devices, shards(): lax.all_to_all(jnp.stack([child_panel] * lax.axis_size('col')), 'col', 0, 0)  49.6 us
    all_gather x1, blocking collectives, spread(): lax.all_gather(own, axis, axis=0, tiled=True)[:len(lines)]  41.5 us
    ppermute x2, waiting for transfers between devices, shifted(): lax.ppermute(value, axis, [(source, source + steps) for source in range(i...  26.9 us
    ppermute x2, starting transfers between devices, shifted(): lax.ppermute(value, axis, [(source, source + steps) for source in range(i...  15.2 us
  transfers between devices with their start and end apart: 8, of which 8 were waited for; matrix products, arithmetic and copies ran while one was open for 1% of the time, Pallas kernels for 0%

profile of v1, /device:TPU:1, one launch (start us, length us, event | category | flops | bytes accessed | tf_op | source)
XLA Modules:
  0.0 612.5 jit_solution(15379036785573674049)
XLA Ops:
  6.5 2.6 stack.2
  9.1 10.2 %all-to-all-start = ((f32[16,1,32,1024]{3,2,1,0:T(8,128)}), f32[16,1,32,1024]{3,2,1,0:T(8,128)S(1)}, u32[]{:S(2)}, u32[]{:S(2)}) async-start(f32[16,1,32,1024]{3,2,1,0:T(8,128)} %stack.2), calls=%async_computation | async-start | bytes 4194304 | tf_op jit(solution)/shard_map/all_to_all | solution.py:101
  19.4 49.6 %all-to-all-done = f32[16,1,32,1024]{3,2,1,0:T(8,128)S(1)} async-done(((f32[16,1,32,1024]{3,2,1,0:T(8,128)}), f32[16,1,32,1024]{3,2,1,0:T(8,128)S(1)}, u32[]{:S(2)}, u32[]{:S(2)}) %all-to-all-start) | async-done | bytes 2097184 | tf_op jit(solution)/shard_map/all_to_all | solution.py:101
  69.0 1.5 broadcast_select_fusion
  70.6 87.6 %all-reduce.7.cloned.1.call-done = f32[512,1024]{1,0:T(8,128)} async-done(((f32[512,1024]{1,0:T(8,128)}), f32[512,1024]{1,0:T(8,128)}) %all-reduce.7.cloned.1.call-update) | async-done | bytes 2097168 | tf_op jit(solution)/shard_map/psum | solution.py:20
  158.3 2.5 copy.15
  160.8 81.6 %all-reduce.9.cloned.1.call-done = f32[512,1024]{1,0:T(8,128)} async-done(((f32[512,1024]{1,0:T(8,128)}), f32[512,1024]{1,0:T(8,128)}) %all-reduce.9.cloned.1.call-update) | async-done | bytes 2097168 | tf_op jit(solution)/shard_map/psum | solution.py:20
  242.4 5.4 fusion.3
  248.9 4.1 collective-permute-start
  253.1 13.7 %collective-permute-done = f32[512,256]{0,1:T(8,128)S(1)} collective-permute-done((f32[512,256]{0,1:T(8,128)S(1)}, f32[512,256]{0,1:T(8,128)S(1)}, u32[]{:S(2)}, u32[]{:S(2)}) %collective-permute-start) | collective-permute-done | bytes 524320 | tf_op jit(solution)/shard_map/ppermute | solution.py:27
  266.8 1.3 pad_maximum_fusion.1
  268.2 1.9 copy.16
  270.0 2.7 convolution_bitcast_fusion
  272.7 1.0 slice.17
  273.7 2.4 copy.17
  276.1 11.1 %collective-permute-start.1 = (f32[256,768]{0,1:T(8,128)}, f32[256,768]{0,1:T(8,128)}, u32[]{:S(2)}, u32[]{:S(2)}) collective-permute-start(f32[256,768]{0,1:T(8,128)} %bitcast.37), channel_id=1, source_target_pairs={{0,16},{16,32},{32,48},{48,64},{64,80},{80,96},{96,112},{112,128},... | collective-permute-start | bytes 2359304 | tf_op jit(solution)/shard_map/ppermute | solution.py:27
  287.2 1.6 copy.18
  288.9 13.2 %collective-permute-done.1 = f32[256,768]{0,1:T(8,128)} collective-permute-done((f32[256,768]{0,1:T(8,128)}, f32[256,768]{0,1:T(8,128)}, u32[]{:S(2)}, u32[]{:S(2)}) %collective-permute-start.1) | collective-permute-done | bytes 786464 | tf_op jit(solution)/shard_map/ppermute | solution.py:27
  302.0 3.2 pad_maximum_fusion
  305.2 2.0 copy.19
  307.2 2.9 fusion
  310.9 7.7 %all_to_all.15 = f32[2,384,768]{2,1,0:T(8,128)S(1)} all-to-all(f32[2,384,768]{2,1,0:T(8,128)S(1)} %bitcast.33), channel_id=1, replica_groups=mesh['sib'=2,'row_0'=8,'row_1'=2,'col'=16] {'sib'}, dimensions={0} | all-to-all | bytes 4718592 | tf_op jit(solution)/shard_map/all_to_all | solution.py:38
  318.6 1.3 reduce_sum.9
  319.9 1.8 add.88
  321.6 2.3 convolution_select_fusion
  324.1 94.5 %reduce-scatter.2.cloned.1.call-done = f32[24,512]{1,0:T(8,128)} async-done(((f32[384,512]{1,0:T(8,128)}), f32[24,512]{1,0:T(8,128)}) %reduce-scatter.2.cloned.1.call-update) | async-done | bytes 49168 | tf_op jit(solution)/shard_map/reduce_scatter | solution.py:52
  418.5 41.5 %all_gather.3 = f32[384,512]{1,0:T(8,128)S(1)} all-gather(f32[24,512]{1,0:T(8,128)} %reduce-scatter.2.cloned.1.call-done), channel_id=1, replica_groups=mesh['sib'=2,'row_0'=8,'row_1'=2,'col'=16] {'col'}, dimensions={0}, use_global_device_ids=true | all-gather | bytes 835584 | tf_op jit(solution)/shard_map/all_gather | solution.py:53
  461.1 78.8 %all-reduce.11.cloned.1.call-done = f32[384,512]{1,0:T(8,128)} async-done(((f32[384,512]{1,0:T(8,128)}), f32[384,512]{1,0:T(8,128)}) %all-reduce.11.cloned.1.call-update) | async-done | bytes 786448 | tf_op jit(solution)/shard_map/psum | solution.py:20
  539.9 56.2 %all-reduce.13.cloned.1.call-done = f32[384,512]{1,0:T(8,128)} async-done(((f32[384,512]{1,0:T(8,128)}), f32[384,512]{1,0:T(8,128)}) %all-reduce.13.cloned.1.call-update) | async-done | bytes 786448 | tf_op jit(solution)/shard_map/psum | solution.py:20
  596.2 1.3 broadcast_in_dim.11
  597.5 5.3 all_to_all.16
  602.8 3.2 fusion.2
  (25 shorter events, 3.1 us)
Async XLA Ops:
  6.5 315.1 %copy-start = (f32[512,512]{1,0:T(8,128)S(1)}, f32[512,512]{1,0:T(8,128)}, u32[]{:S(2)}) copy-start(f32[512,512]{1,0:T(8,128)} %param.9) | copy-start | bytes 3145732
  9.1 59.9 %all-to-all-start = ((f32[16,1,32,1024]{3,2,1,0:T(8,128)}), f32[16,1,32,1024]{3,2,1,0:T(8,128)S(1)}, u32[]{:S(2)}, u32[]{:S(2)}) async-start(f32[16,1,32,1024]{3,2,1,0:T(8,128)} %stack.2), calls=%async_computation | async-start | bytes 4194304 | tf_op jit(solution)/shard_map/all_to_all | solution.py:101
  19.4 138.9 %all-reduce.7.cloned.1.call-start = ((), (), s32[]{:S(2)}) async-start(), calls=%async_computation.4 | async-start | bytes 4194304 | tf_op jit(solution)/shard_map/psum | solution.py:20
  70.5 171.9 %all-reduce.9.cloned.1.call-start = ((), (), s32[]{:S(2)}) async-start(), calls=%async_computation.5 | async-start | bytes 4194304 | tf_op jit(solution)/shard_map/psum | solution.py:20
  158.2 260.3 %reduce-scatter.2.cloned.1.call-start = ((), (), s32[]{:S(2)}) async-start(), calls=%async_computation.6 | async-start | bytes 835584 | tf_op jit(solution)/shard_map/reduce_scatter | solution.py:52
  242.4 10.5 %copy-start.2 = (s32[2,64]{1,0:T(2,128)S(1)}, s32[2,64]{1,0:T(2,128)}, u32[]{:S(2)}) copy-start(s32[2,64]{1,0:T(2,128)} %param.7) | copy-start | bytes 1540
  247.9 1.0 copy-start.1
  248.9 17.9 %collective-permute-start = (f32[512,256]{0,1:T(8,128)S(1)}, f32[512,256]{0,1:T(8,128)S(1)}, u32[]{:S(2)}, u32[]{:S(2)}) collective-permute-start(f32[512,256]{0,1:T(8,128)S(1)} %slice.16), channel_id=1, source_target_pairs={{0,1},{1,2},{2,3},{3,4},{4,5},{5,6},{6,7},{7,8},{8,9},{9,10},{10,1... | collective-permute-start | bytes 1572872 | tf_op jit(solution)/shard_map/ppermute | solution.py:27
  276.1 25.9 %collective-permute-start.1 = (f32[256,768]{0,1:T(8,128)}, f32[256,768]{0,1:T(8,128)}, u32[]{:S(2)}, u32[]{:S(2)}) collective-permute-start(f32[256,768]{0,1:T(8,128)} %bitcast.37), channel_id=1, source_target_pairs={{0,16},{16,32},{32,48},{48,64},{64,80},{80,96},{96,112},{112,128},... | collective-permute-start | bytes 2359304 | tf_op jit(solution)/shard_map/ppermute | solution.py:27
  324.0 215.9 %all-reduce.11.cloned.1.call-start = ((), (), s32[]{:S(2)}) async-start(), calls=%async_computation.7 | async-start | bytes 1572864 | tf_op jit(solution)/shard_map/psum | solution.py:20
  461.0 135.1 %all-reduce.13.cloned.1.call-start = ((), (), s32[]{:S(2)}) async-start(), calls=%async_computation.8 | async-start | bytes 1572864 | tf_op jit(solution)/shard_map/psum | solution.py:20
Sparse Core Ops, SparseCore 0:
  70.7 87.5 all-reduce.6
  161.1 81.2 all-reduce.8
  324.1 94.3 reduce-scatter.1
  461.1 78.6 all-reduce.10
  542.6 53.5 all-reduce.12
